TPU v7x, 32 devices: a whole 2x2x4 slice. The times are simulated.
32 devices in a mesh: seq: 8 (over z, y), chan: 4 (over x, core).
Axes of the slice: x: 2, y: 2, z: 4, core: 2. Of those that a mesh axis runs over, the one named last changes fastest.
Arguments:
- query_gate: float32 [16, 65536], P('chan', 'seq'), may hold values from -6 to 6
- key_gate: float32 [16, 65536], P('chan', 'seq'), may hold values from -6 to 6
- value_input: float32 [16, 65536], P('chan', 'seq'), may hold values from -6 to 6
- filter_taps: float32 [4, 65536], P(None, ('seq', 'chan')), may hold values from -2 to 2
- cotangent: float32 [16, 65536], P('chan', 'seq'), may hold values from -6 to 6
Outputs:
- query_grad: float32 [16, 65536], P('chan', 'seq')
- key_grad: float32 [16, 65536], P('chan', 'seq')
- value_grad: float32 [16, 65536], P('chan', 'seq')
All inputs are finite; a program needn't handle non-finite values.
Results may differ from a plain program's by a relative error of at most 0.00013.
Values sent between devices are 32-bit elements; how exact they have to be, the bound alone decides.
A program may use at most 64 MiB of HBM per device.

v0:
```python
from functools import partial
import math

import jax
import jax.numpy as jnp
import numpy as np
from jax import lax
from jax.experimental import pallas as pl
from jax.experimental.pallas import tpu as pltpu
from jax.sharding import PartitionSpec as P

MESH = pl.DeviceIdType.MESH
SIDE = 256
LANES = 128
VMEM_BYTES = 63 * 1024 * 1024


def fourier_tables():
    total = SIDE * SIDE
    index = np.arange(SIDE, dtype=np.float64)
    outer = 2.0 * np.pi * np.outer(index + 0.25, index) / SIDE
    first = np.concatenate([np.cos(outer), -np.sin(outer)], axis=0)
    last = first.T / total
    inner = 2.0 * np.pi * (np.outer(index, index) % SIDE) / SIDE
    twist = 2.0 * np.pi * np.outer(index + 0.25, index) / total
    tables = (first, np.cos(inner), np.sin(inner), last, np.cos(twist), -np.sin(twist))
    return tuple(table.astype(np.float32) for table in tables)


def split(value):
    high = value.astype(jnp.bfloat16)
    low = (value - high.astype(jnp.float32)).astype(jnp.bfloat16)
    return high, low


def mul(left, right):
    dot = partial(jnp.dot, preferred_element_type=jnp.float32)
    return dot(left[0], right[0]) + (dot(left[0], right[1]) + dot(left[1], right[0]))


def row_kernel(
    blocks, groups, k_hbm, v_hbm, q_hbm, c_hbm, taps_hbm,
    first_hbm, cos_hbm, sin_hbm, last_hbm, turn_re_hbm, turn_im_hbm, out_ref,
    k_ref, v_ref, q_ref, c_ref, taps_ref, first_ref, cos_ref, sin_ref, last_ref, turn_re_ref, turn_im_ref,
    pieces, tap_pieces, rows, side, filt, result, side_result, back,
    first_hi, first_lo, mid_hi, mid_lo, inv_hi, inv_lo, last_hi, last_lo,
    load_sem, tap_send, tap_recv, slab_send, slab_recv, in_send, in_recv, out_send, out_recv,
    side_send, side_recv, home_send, home_recv,
):
    me = lax.axis_index("seq")
    col = lax.axis_index("chan")
    count = k_ref.shape[0]
    parts = SIDE // LANES
    near = blocks // 2
    base = (me // near) * near
    local = lax.rem(me, near)
    depth = SIDE // 2

    sources = (taps_hbm, k_hbm, v_hbm, c_hbm, q_hbm, first_hbm, cos_hbm, sin_hbm, turn_re_hbm, turn_im_hbm, last_hbm)
    targets = (taps_ref, k_ref, v_ref, c_ref, q_ref, first_ref, cos_ref, sin_ref, turn_re_ref, turn_im_ref, last_ref)
    loads = [
        pltpu.make_async_copy(source, target, load_sem.at[place])
        for place, (source, target) in enumerate(zip(sources, targets))
    ]
    for load in loads:
        load.start()

    barrier = pltpu.get_barrier_semaphore()
    for step in range(1, blocks):
        pl.semaphore_signal(barrier, inc=1, device_id=(lax.rem(me + step, blocks), col), device_id_type=MESH)
    for step in range(1, groups):
        pl.semaphore_signal(barrier, inc=1, device_id=(me, lax.rem(col + step, groups)), device_id_type=MESH)

    def span(row, part):
        return slice(row * SIDE + part * LANES, row * SIDE + (part + 1) * LANES)

    loads[0].wait()
    for part in range(parts):
        for row in range(taps_ref.shape[1] // SIDE):
            tap_pieces[:, part, row, :] = taps_ref[:, span(row, part)]
    for load in loads[1:5]:
        load.wait()
    for part in range(parts):
        for row in range(k_ref.shape[1] // SIDE):
            tokens = span(row, part)
            pieces[:count, part, row, :] = k_ref[:, tokens] * v_ref[:, tokens]
            pieces[count:, part, row, :] = c_ref[:, tokens] * q_ref[:, tokens]

    pl.semaphore_wait(barrier, blocks + groups - 2)

    tap_copies, slab_copies, side_copies, home_copies = [], [], [], []
    in_copies, out_copies = [[] for _ in range(parts)], [[] for _ in range(parts)]
    for step in range(1, blocks):
        target = lax.rem(me + step, blocks)
        copy = pltpu.make_async_remote_copy(
            src_ref=tap_pieces.at[lax.rem(target, count)], dst_ref=filt.at[me, col],
            send_sem=tap_send.at[step], recv_sem=tap_recv.at[step],
            device_id=(target, col), device_id_type=MESH,
        )
        copy.start()
        tap_copies.append(copy)
    for part in range(parts):
        for step in range(1, blocks):
            target = lax.rem(me + step, blocks)
            copy = pltpu.make_async_remote_copy(
                src_ref=pieces.at[lax.rem(target + near, blocks), part], dst_ref=rows.at[part, me],
                send_sem=in_send.at[part, step], recv_sem=in_recv.at[part, step],
                device_id=(target, col), device_id_type=MESH,
            )
            copy.start()
            in_copies[part].append(copy)
        for step in range(1, near if part == 0 else 1):
            target = base + lax.rem(me + step, near)
            copy = pltpu.make_async_remote_copy(
                src_ref=pieces.at[target], dst_ref=side.at[local],
                send_sem=side_send.at[step], recv_sem=side_recv.at[step],
                device_id=(target, col), device_id_type=MESH,
            )
            copy.start()
            side_copies.append(copy)
    side[local] = pieces[me]
    filt[me, col] = tap_pieces[lax.rem(me, count)]
    for part in range(parts):
        rows[part, me] = pieces[lax.rem(me + near, blocks), part]

    for copy in tap_copies:
        copy.wait_recv()
    for step in range(1, groups):
        copy = pltpu.make_async_remote_copy(
            src_ref=filt.at[:, col], dst_ref=filt.at[:, col],
            send_sem=slab_send.at[step], recv_sem=slab_recv.at[step],
            device_id=(me, lax.rem(col + step, groups)), device_id_type=MESH,
        )
        copy.start()
        slab_copies.append(copy)

    for load in loads[5:]:
        load.wait()
    first_hi[...], first_lo[...] = split(first_ref[...])
    last_hi[...], last_lo[...] = split(last_ref[...])
    cosines, sines = split(cos_ref[...]), split(sin_ref[...])
    for part in range(parts):
        cut = slice(part * LANES, (part + 1) * LANES)
        real_rows = slice(2 * part * LANES, (2 * part + 1) * LANES)
        imag_rows = slice((2 * part + 1) * LANES, (2 * part + 2) * LANES)
        for mid, inv, cosine, sine in zip((mid_hi, mid_lo), (inv_hi, inv_lo), cosines, sines):
            mid[real_rows, :SIDE] = cosine[cut]
            mid[real_rows, SIDE:] = -sine[cut]
            mid[imag_rows, :SIDE] = sine[cut]
            mid[imag_rows, SIDE:] = cosine[cut]
            inv[part, :SIDE, :LANES] = cosine[:, cut]
            inv[part, :SIDE, LANES:] = sine[:, cut]
            inv[part, SIDE:, :LANES] = -sine[:, cut]
            inv[part, SIDE:, LANES:] = cosine[:, cut]

    def part_spectrum(part, signal):
        cut = slice(part * LANES, (part + 1) * LANES)
        wide = slice(part * SIDE, (part + 1) * SIDE)
        held = slice(0, signal.shape[0])
        mixed = mul((first_hi[:, held], first_lo[:, held]), split(signal))
        real, imag = mixed[:SIDE], mixed[SIDE:]
        turn_re, turn_im = turn_re_ref[:, cut], turn_im_ref[:, cut]
        twisted = jnp.concatenate(
            [real * turn_re - imag * turn_im, real * turn_im + imag * turn_re], axis=1
        )
        return mul(split(twisted), (mid_hi[wide], mid_lo[wide]))

    def row_spectrum(part):
        for copy in in_copies[part]:
            copy.wait_recv()
        return part_spectrum(part, rows[part].reshape(SIDE, LANES))

    def product(total, tap_re, tap_im):
        real, imag = total[:, :SIDE], total[:, SIDE:]
        return split(jnp.concatenate([real * tap_re - imag * tap_im, real * tap_im + imag * tap_re], axis=1))

    def part_tokens(part, joined, first_row):
        cut = slice(part * LANES, (part + 1) * LANES)
        coarse = mul(joined, (inv_hi[part], inv_lo[part]))
        real, imag = coarse[:, :LANES], coarse[:, LANES:]
        turn_re, turn_im = turn_re_ref[:, cut], turn_im_ref[:, cut]
        level = jnp.concatenate(
            [real * turn_re + imag * turn_im, imag * turn_re - real * turn_im], axis=0
        )
        kept = pl.ds(first_row, depth)
        return mul((last_hi[kept, :], last_lo[kept, :]), split(level))

    row_total = row_spectrum(0)
    for copy in slab_copies:
        copy.wait_recv()
    tap_total = part_spectrum(0, filt[:, :, 0].reshape(SIDE, LANES))
    for part in range(1, parts):
        tap_total += part_spectrum(part, filt[:, :, part].reshape(SIDE, LANES))
    tap_re = tap_total[:, :SIDE]
    tap_im = tap_total[:, SIDE:] * jnp.where(me < near, -1.0, 1.0)

    for copy in side_copies:
        copy.wait_recv()
    side_total = part_spectrum(0, side[:, 0].reshape(depth, LANES))
    for part in range(1, parts):
        side_total += part_spectrum(part, side[:, part].reshape(depth, LANES))
    joined = product(side_total, tap_re, -tap_im)
    for part in range(parts):
        side_result[:, part] = part_tokens(part, joined, 0).reshape(near, *side_result.shape[2:])
    for step in range(1, near):
        target = lax.rem(me + step, near)
        copy = pltpu.make_async_remote_copy(
            src_ref=side_result.at[target], dst_ref=back.at[me],
            send_sem=home_send.at[step], recv_sem=home_recv.at[step],
            device_id=(base + target, col), device_id_type=MESH,
        )
        copy.start()
        home_copies.append(copy)
    back[me] = side_result[local]

    for part in range(1, parts):
        row_total += row_spectrum(part)
    joined = product(row_total, tap_re, tap_im)
    place = lax.rem(me + near, blocks)
    for part in range(parts):
        result[part] = part_tokens(part, joined, pl.multiple_of((me // near) * depth, depth)).reshape(result.shape[1:])
        for step in range(1, near):
            target = lax.rem(me + step, near)
            copy = pltpu.make_async_remote_copy(
                src_ref=result.at[part, target], dst_ref=back.at[place, part],
                send_sem=out_send.at[part, step], recv_sem=out_recv.at[part, step],
                device_id=(base + target, col), device_id_type=MESH,
            )
            copy.start()
            out_copies[part].append(copy)
        back[place, part] = result[part, local]
    for copy in home_copies:
        copy.wait_recv()
    for part in range(parts):
        for copy in out_copies[part]:
            copy.wait_recv()
        for row in range(back.shape[2]):
            out_ref[:, span(row, part)] = back[:, part, row, :]
    for copy in tap_copies + sum(in_copies, []) + slab_copies + side_copies + home_copies + sum(out_copies, []):
        copy.wait_send()


def rows_on_device(query_gate, key_gate, value_input, filter_taps, cotangent):
    count, width = query_gate.shape
    blocks = lax.axis_size("seq")
    groups = lax.axis_size("chan")
    high = width // SIDE
    near = blocks // 2
    parts = SIDE // LANES
    tables = fourier_tables()
    f32, bf16 = jnp.float32, jnp.bfloat16
    operands = (key_gate, value_input, query_gate, cotangent, filter_taps, *[jnp.asarray(table) for table in tables])
    sums = pl.pallas_call(
        partial(row_kernel, blocks, groups),
        out_shape=jax.ShapeDtypeStruct((blocks, width), f32),
        in_specs=[pl.BlockSpec(memory_space=pl.ANY)] * len(operands),
        out_specs=pl.BlockSpec(memory_space=pltpu.VMEM),
        scratch_shapes=[
            *[pltpu.VMEM(operand.shape, f32) for operand in operands],
            pltpu.VMEM((blocks, parts, high, LANES), f32),
            pltpu.VMEM((count, parts, high // groups, LANES), f32),
            pltpu.VMEM((parts, blocks, high, LANES), f32),
            pltpu.VMEM((near, parts, high, LANES), f32),
            pltpu.VMEM((blocks, groups, parts, high // groups, LANES), f32),
            pltpu.VMEM((parts, near, high, LANES), f32),
            pltpu.VMEM((near, parts, high, LANES), f32),
            pltpu.VMEM((blocks, parts, high, LANES), f32),
            pltpu.VMEM((2 * SIDE, SIDE), bf16),
            pltpu.VMEM((2 * SIDE, SIDE), bf16),
            pltpu.VMEM((2 * SIDE, 2 * SIDE), bf16),
            pltpu.VMEM((2 * SIDE, 2 * SIDE), bf16),
            pltpu.VMEM((parts, 2 * SIDE, SIDE), bf16),
            pltpu.VMEM((parts, 2 * SIDE, SIDE), bf16),
            pltpu.VMEM((SIDE, 2 * SIDE), bf16),
            pltpu.VMEM((SIDE, 2 * SIDE), bf16),
            pltpu.SemaphoreType.DMA((len(operands),)),
            pltpu.SemaphoreType.DMA((blocks,)),
            pltpu.SemaphoreType.DMA((blocks,)),
            pltpu.SemaphoreType.DMA((groups,)),
            pltpu.SemaphoreType.DMA((groups,)),
            pltpu.SemaphoreType.DMA((parts, blocks)),
            pltpu.SemaphoreType.DMA((parts, blocks)),
            pltpu.SemaphoreType.DMA((parts, blocks)),
            pltpu.SemaphoreType.DMA((parts, blocks)),
            *[pltpu.SemaphoreType.DMA((near,))] * 4,
        ],
        compiler_params=pltpu.CompilerParams(
            collective_id=0, has_side_effects=True, vmem_limit_bytes=VMEM_BYTES
        ),
    )(*operands)
    convolved, gated_grad = sums[:count], sums[count:]
    return (cotangent * convolved, gated_grad * value_input, gated_grad * key_gate)


def one_row_each(query_gate, filter_taps):
    count, width = query_gate.shape
    blocks = lax.axis_size("seq")
    groups = lax.axis_size("chan")
    return (
        blocks == 2 * count
        and filter_taps.shape[0] == count
        and blocks * width == SIDE * SIDE
        and width % (8 * groups * SIDE) == 0
    )


def phase_table(row_count, column_count, offset, period, direction):
    row_index = lax.broadcasted_iota(jnp.int32, (row_count, column_count), 0)
    column_index = lax.broadcasted_iota(jnp.int32, (row_count, column_count), 1)
    phases = row_index * (column_index + offset) % period
    angles = phases.astype(jnp.float32) * (direction * 2.0 * math.pi / period)
    return (jnp.cos(angles), jnp.sin(angles))


def complex_mix(formula, table_real, table_imag, data_real, data_imag):
    product = partial(jnp.einsum, formula, precision=lax.Precision.HIGHEST)
    return (
        product(table_real, data_real) - product(table_imag, data_imag),
        product(table_real, data_imag) + product(table_imag, data_real),
    )


def regroup_tokens(signal):
    return lax.all_to_all(signal, "seq", split_axis=1, concat_axis=1, tiled=True)


def regroup_spectrum(part_real, part_imag):
    return (
        lax.all_to_all(part_real, "seq", split_axis=1, concat_axis=1, tiled=True),
        lax.all_to_all(part_imag, "seq", split_axis=1, concat_axis=1, tiled=True),
    )


def finish_forward(moved_real, moved_imag, blocks, width, tokens):
    outer_real, outer_imag = phase_table(blocks, blocks, 0, blocks, -1.0)
    coarse_real, coarse_imag = complex_mix(
        "ur,crjq->cujq", outer_real, outer_imag, moved_real, moved_imag
    )
    shift_real, shift_imag = phase_table(blocks, width, 0, tokens, -1.0)
    shift_real = shift_real[None, :, None, :]
    shift_imag = shift_imag[None, :, None, :]
    twisted_real = coarse_real * shift_real - coarse_imag * shift_imag
    twisted_imag = coarse_real * shift_imag + coarse_imag * shift_real
    inner_real, inner_imag = phase_table(width, width, 0, width, -1.0)
    return complex_mix("qv,cujq->cujv", inner_real, inner_imag, twisted_real, twisted_imag)


def start_inverse(spectrum_real, spectrum_imag, blocks, width, tokens):
    inner_real, inner_imag = phase_table(width, width, 0, width, 1.0)
    fine_real, fine_imag = complex_mix(
        "vq,cujv->cujq", inner_real, inner_imag, spectrum_real, spectrum_imag
    )
    shift_real, shift_imag = phase_table(blocks, width, 0, tokens, 1.0)
    shift_real = shift_real[None, :, None, :]
    shift_imag = shift_imag[None, :, None, :]
    untwisted_real = fine_real * shift_real - fine_imag * shift_imag
    untwisted_imag = fine_real * shift_imag + fine_imag * shift_real
    outer_real, outer_imag = phase_table(blocks, blocks, 0, blocks, 1.0)
    return complex_mix("ru,cujq->crjq", outer_real, outer_imag, untwisted_real, untwisted_imag)


def forward_spectrum(signal):
    count, tokens = signal.shape
    blocks = lax.axis_size("seq")
    width = tokens // blocks
    freqs = 2 * blocks
    period = freqs * tokens
    rank = lax.axis_index("seq")
    gathered = regroup_tokens(signal.reshape(count, blocks, width))
    product = partial(jnp.einsum, "kp,cpq->ckq", precision=lax.Precision.HIGHEST)
    anchor = rank * width
    first_real, first_imag = phase_table(freqs, blocks, 0, freqs, -1.0)
    mixed_real = product(first_real, gathered)
    mixed_imag = product(first_imag, gathered)
    turn_real, turn_imag = phase_table(freqs, width, anchor, period, -1.0)
    moved_real, moved_imag = regroup_spectrum(
        mixed_real * turn_real - mixed_imag * turn_imag,
        mixed_real * turn_imag + mixed_imag * turn_real,
    )
    moved_real = moved_real.reshape(count, blocks, 2, width)
    moved_imag = moved_imag.reshape(count, blocks, 2, width)
    return finish_forward(moved_real, moved_imag, blocks, width, tokens)


def inverse_spectrum(spectrum_real, spectrum_imag):
    count, blocks, per_device, width = spectrum_real.shape
    tokens = blocks * width
    freqs = 2 * blocks
    period = freqs * tokens
    rank = lax.axis_index("seq")
    spread_real, spread_imag = start_inverse(spectrum_real, spectrum_imag, blocks, width, tokens)
    product = partial(jnp.einsum, "kp,ckq->cpq", precision=lax.Precision.HIGHEST)
    anchor = rank * width
    moved_real, moved_imag = regroup_spectrum(
        spread_real.reshape(count, blocks * per_device, width),
        spread_imag.reshape(count, blocks * per_device, width),
    )
    turn_real, turn_imag = phase_table(freqs, width, anchor, period, 1.0)
    level_real = moved_real * turn_real - moved_imag * turn_imag
    level_imag = moved_real * turn_imag + moved_imag * turn_real
    first_real, first_imag = phase_table(freqs, blocks, 0, freqs, 1.0)
    rebuilt = (product(first_real, level_real) - product(first_imag, level_imag)) * (1.0 / period)
    return regroup_tokens(rebuilt).reshape(count, tokens)


def on_device(query_gate, key_gate, value_input, filter_taps, cotangent):
    if one_row_each(query_gate, filter_taps):
        return rows_on_device(query_gate, key_gate, value_input, filter_taps, cotangent)
    block_taps = lax.all_gather(filter_taps, "chan", axis=1, tiled=True)
    filter_real, filter_imag = forward_spectrum(block_taps)
    gated = key_gate * value_input
    weighted = cotangent * query_gate
    gated_real, gated_imag = forward_spectrum(gated)
    convolved = inverse_spectrum(
        gated_real * filter_real - gated_imag * filter_imag,
        gated_real * filter_imag + gated_imag * filter_real,
    )
    weighted_real, weighted_imag = forward_spectrum(weighted)
    gated_grad = inverse_spectrum(
        weighted_real * filter_real + weighted_imag * filter_imag,
        weighted_imag * filter_real - weighted_real * filter_imag,
    )
    return (cotangent * convolved, gated_grad * value_input, gated_grad * key_gate)


def solution(mesh):
    in_specs = (
        P("chan", "seq"),
        P("chan", "seq"),
        P("chan", "seq"),
        P(None, ("seq", "chan")),
        P("chan", "seq"),
    )
    out_specs = (P("chan", "seq"), P("chan", "seq"), P("chan", "seq"))
    return jax.shard_map(
        on_device, mesh=mesh, in_specs=in_specs, out_specs=out_specs, check_vma=False
    )
```

profile of v0, /device:TPU:0, one launch (start us, length us, event | category | flops | bytes accessed | tf_op | source)
XLA Modules:
  0.0 27.9 jit_solution(11483264884062401644)
XLA Ops:
  0.6 0.0 copy-start.2
  0.6 0.0 copy-start.1
  0.7 0.0 copy-start
  0.7 25.4 %shard_map.130 = f32[8,8192]{1,0:T(8,128)} custom-call(f32[4,8192]{1,0:T(4,128)} %k_hbm.1, f32[4,8192]{1,0:T(4,128)} %v_hbm.1, f32[4,8192]{1,0:T(4,128)} %q_hbm.1, f32[4,8192]{1,0:T(4,128)} %c_hbm.1, f32[4,2048]{1,0:T(4,128)} %taps_hbm.1, f32[512,256]{1,0:T(8,128)} %constant.12.clone.first_hbm, f32[256,256]{1,0:T(8,128)} %constant.13.clone.cos_hbm, ...), custom_call_target="tpu_custom_call" | custom-call | tf_op jit(solution)/shard_map/pallas_call | solution.py:253
  26.1 0.0 copy-done.2
  26.1 0.0 copy-done.1
  26.1 0.0 copy-done
  26.1 1.8 %slice_multiply_fusion.1 = (f32[4,8192]{1,0:T(4,128)}, f32[4,8192]{1,0:T(4,128)}, f32[4,8192]{1,0:T(4,128)}) fusion(f32[4,8192]{1,0:T(4,128)S(1)} %copy-done, f32[8,8192]{1,0:T(8,128)} %shard_map.130, f32[4,8192]{1,0:T(4,128)S(1)} %copy-done.1, f32[4,8192]{1,0:T(4,128)S(1)} %copy-done.2), kind=kLoop, calls=%fused_computation.1 | loop fusion | flops 98304 | bytes 1048576 | tf_op jit(solution)/shard_map/mul | solution.py:292
Async XLA Ops:
  0.6 25.5 %copy-start.2 = (f32[4,8192]{1,0:T(4,128)S(1)}, f32[4,8192]{1,0:T(4,128)}, u32[]{:S(2)}) copy-start(f32[4,8192]{1,0:T(4,128)} %c_hbm.1) | copy-start | bytes 393220
  0.6 25.5 %copy-start.1 = (f32[4,8192]{1,0:T(4,128)S(1)}, f32[4,8192]{1,0:T(4,128)}, u32[]{:S(2)}) copy-start(f32[4,8192]{1,0:T(4,128)} %v_hbm.1) | copy-start | bytes 393220
  0.7 25.5 %copy-start = (f32[4,8192]{1,0:T(4,128)S(1)}, f32[4,8192]{1,0:T(4,128)}, u32[]{:S(2)}) copy-start(f32[4,8192]{1,0:T(4,128)} %k_hbm.1) | copy-start | bytes 393220
where the time goes:
time: 28.1 us; the launch traced here: 27.9 us
  Pallas kernels  25.4 us (90%)
  other arithmetic  1.83 us (7%)
  between operations  0.69 us (2%)
    pallas_call x1, Pallas kernels, rows_on_device(): pl.pallas_call(partial(row_kernel, blocks, groups), out_shape=jax.ShapeDt...  25.4 us
    mul x1, other arithmetic, rows_on_device(): gated_grad * key_gate  1.83 us

commit v1 on v0

--- a/solution.py
+++ b/solution.py
@@ -21,9 +21,15 @@
     outer = 2.0 * np.pi * np.outer(index + 0.25, index) / SIDE
     first = np.concatenate([np.cos(outer), -np.sin(outer)], axis=0)
     last = first.T / total
-    inner = 2.0 * np.pi * (np.outer(index, index) % SIDE) / SIDE
+    inner_index = np.arange(LANES, dtype=np.float64)
+    inner = 2.0 * np.pi * (np.outer(inner_index, inner_index) % LANES) / LANES
+    cosine, sine = np.cos(inner), np.sin(inner)
+    middle = np.block([[cosine, -sine], [sine, cosine]])
+    inverse = np.block([[cosine, sine], [-sine, cosine]])
     twist = 2.0 * np.pi * np.outer(index + 0.25, index) / total
-    tables = (first, np.cos(inner), np.sin(inner), last, np.cos(twist), -np.sin(twist))
+    odd = 2.0 * np.pi * inner_index / SIDE
+    shift = np.stack([np.cos(odd), -np.sin(odd)] * 4)
+    tables = (first, middle, inverse, last, np.cos(twist), -np.sin(twist), shift)
     return tuple(table.astype(np.float32) for table in tables)
 
 
@@ -33,17 +39,26 @@
     return high, low
 
 
+def stack_left(value, axis=1):
+    high, low = split(value)
+    return jnp.concatenate([high, high, low], axis=axis)
+
+
+def stack_right(value, axis=0):
+    high, low = split(value)
+    return jnp.concatenate([high, low, high], axis=axis)
+
+
 def mul(left, right):
-    dot = partial(jnp.dot, preferred_element_type=jnp.float32)
-    return dot(left[0], right[0]) + (dot(left[0], right[1]) + dot(left[1], right[0]))
+    return jnp.dot(left, right, preferred_element_type=jnp.float32)
 
 
 def row_kernel(
     blocks, groups, k_hbm, v_hbm, q_hbm, c_hbm, taps_hbm,
-    first_hbm, cos_hbm, sin_hbm, last_hbm, turn_re_hbm, turn_im_hbm, out_ref,
-    k_ref, v_ref, q_ref, c_ref, taps_ref, first_ref, cos_ref, sin_ref, last_ref, turn_re_ref, turn_im_ref,
+    first_hbm, mid_hbm, inv_hbm, last_hbm, turn_re_hbm, turn_im_hbm, shift_hbm, out_ref,
+    k_ref, v_ref, q_ref, c_ref, taps_ref, first_ref, mid_ref, inv_ref, last_ref, turn_re_ref, turn_im_ref, shift_ref,
     pieces, tap_pieces, rows, side, filt, result, side_result, back,
-    first_hi, first_lo, mid_hi, mid_lo, inv_hi, inv_lo, last_hi, last_lo,
+    first_all, mid_all, inv_all, last_all,
     load_sem, tap_send, tap_recv, slab_send, slab_recv, in_send, in_recv, out_send, out_recv,
     side_send, side_recv, home_send, home_recv,
 ):
@@ -56,8 +71,8 @@
     local = lax.rem(me, near)
     depth = SIDE // 2
 
-    sources = (taps_hbm, k_hbm, v_hbm, c_hbm, q_hbm, first_hbm, cos_hbm, sin_hbm, turn_re_hbm, turn_im_hbm, last_hbm)
-    targets = (taps_ref, k_ref, v_ref, c_ref, q_ref, first_ref, cos_ref, sin_ref, turn_re_ref, turn_im_ref, last_ref)
+    sources = (taps_hbm, k_hbm, v_hbm, c_hbm, q_hbm, first_hbm, mid_hbm, inv_hbm, turn_re_hbm, turn_im_hbm, last_hbm, shift_hbm)
+    targets = (taps_ref, k_ref, v_ref, c_ref, q_ref, first_ref, mid_ref, inv_ref, turn_re_ref, turn_im_ref, last_ref, shift_ref)
     loads = [
         pltpu.make_async_copy(source, target, load_sem.at[place])
         for place, (source, target) in enumerate(zip(sources, targets))
@@ -136,72 +151,69 @@
 
     for load in loads[5:]:
         load.wait()
-    first_hi[...], first_lo[...] = split(first_ref[...])
-    last_hi[...], last_lo[...] = split(last_ref[...])
-    cosines, sines = split(cos_ref[...]), split(sin_ref[...])
-    for part in range(parts):
+    first_all[...] = stack_left(first_ref[...])
+    last_all[...] = stack_left(last_ref[...])
+    mid_all[...] = stack_right(mid_ref[...])
+    inv_all[...] = stack_right(inv_ref[...])
+    shift_re, shift_im = shift_ref[0:1, :], shift_ref[1:2, :]
+
+    def twisted(mixed, part):
         cut = slice(part * LANES, (part + 1) * LANES)
-        real_rows = slice(2 * part * LANES, (2 * part + 1) * LANES)
-        imag_rows = slice((2 * part + 1) * LANES, (2 * part + 2) * LANES)
-        for mid, inv, cosine, sine in zip((mid_hi, mid_lo), (inv_hi, inv_lo), cosines, sines):
-            mid[real_rows, :SIDE] = cosine[cut]
-            mid[real_rows, SIDE:] = -sine[cut]
-            mid[imag_rows, :SIDE] = sine[cut]
-            mid[imag_rows, SIDE:] = cosine[cut]
-            inv[part, :SIDE, :LANES] = cosine[:, cut]
-            inv[part, :SIDE, LANES:] = sine[:, cut]
-            inv[part, SIDE:, :LANES] = -sine[:, cut]
-            inv[part, SIDE:, LANES:] = cosine[:, cut]
-
-    def part_spectrum(part, signal):
-        cut = slice(part * LANES, (part + 1) * LANES)
-        wide = slice(part * SIDE, (part + 1) * SIDE)
-        held = slice(0, signal.shape[0])
-        mixed = mul((first_hi[:, held], first_lo[:, held]), split(signal))
         real, imag = mixed[:SIDE], mixed[SIDE:]
         turn_re, turn_im = turn_re_ref[:, cut], turn_im_ref[:, cut]
-        twisted = jnp.concatenate(
-            [real * turn_re - imag * turn_im, real * turn_im + imag * turn_re], axis=1
+        return real * turn_re - imag * turn_im, real * turn_im + imag * turn_re
+
+    def spectrum(near_part, far_part):
+        (near_re, near_im), (far_re, far_im) = near_part, far_part
+        gap_re, gap_im = near_re - far_re, near_im - far_im
+        even = jnp.concatenate([near_re + far_re, near_im + far_im], axis=1)
+        odd = jnp.concatenate(
+            [gap_re * shift_re - gap_im * shift_im, gap_re * shift_im + gap_im * shift_re], axis=1
         )
-        return mul(split(twisted), (mid_hi[wide], mid_lo[wide]))
-
-    def row_spectrum(part):
+        total = mul(stack_left(jnp.concatenate([even, odd], axis=0)), mid_all[...])
+        return total[:, :LANES], total[:, LANES:]
+
+    def levels(row_re, row_im, tap_re, tap_im):
+        joined = jnp.concatenate(
+            [row_re * tap_re - row_im * tap_im, row_re * tap_im + row_im * tap_re], axis=1
+        )
+        coarse = mul(stack_left(joined), inv_all[...])
+        even_re, even_im = coarse[:SIDE, :LANES], coarse[:SIDE, LANES:]
+        odd_re, odd_im = coarse[SIDE:, :LANES], coarse[SIDE:, LANES:]
+        gap_re = odd_re * shift_re + odd_im * shift_im
+        gap_im = odd_im * shift_re - odd_re * shift_im
+        found = []
+        for part, real, imag in ((0, even_re + gap_re, even_im + gap_im), (1, even_re - gap_re, even_im - gap_im)):
+            cut = slice(part * LANES, (part + 1) * LANES)
+            turn_re, turn_im = turn_re_ref[:, cut], turn_im_ref[:, cut]
+            found.append(jnp.concatenate(
+                [real * turn_re + imag * turn_im, imag * turn_re - real * turn_im], axis=0
+            ))
+        return found
+
+    def row_part(part):
         for copy in in_copies[part]:
             copy.wait_recv()
-        return part_spectrum(part, rows[part].reshape(SIDE, LANES))
-
-    def product(total, tap_re, tap_im):
-        real, imag = total[:, :SIDE], total[:, SIDE:]
-        return split(jnp.concatenate([real * tap_re - imag * tap_im, real * tap_im + imag * tap_re], axis=1))
-
-    def part_tokens(part, joined, first_row):
-        cut = slice(part * LANES, (part + 1) * LANES)
-        coarse = mul(joined, (inv_hi[part], inv_lo[part]))
-        real, imag = coarse[:, :LANES], coarse[:, LANES:]
-        turn_re, turn_im = turn_re_ref[:, cut], turn_im_ref[:, cut]
-        level = jnp.concatenate(
-            [real * turn_re + imag * turn_im, imag * turn_re - real * turn_im], axis=0
-        )
-        kept = pl.ds(first_row, depth)
-        return mul((last_hi[kept, :], last_lo[kept, :]), split(level))
-
-    row_total = row_spectrum(0)
+        return twisted(mul(first_all[...], stack_right(rows[part].reshape(SIDE, LANES))), part)
+
+    row_near = row_part(0)
     for copy in slab_copies:
         copy.wait_recv()
-    tap_total = part_spectrum(0, filt[:, :, 0].reshape(SIDE, LANES))
-    for part in range(1, parts):
-        tap_total += part_spectrum(part, filt[:, :, part].reshape(SIDE, LANES))
-    tap_re = tap_total[:, :SIDE]
-    tap_im = tap_total[:, SIDE:] * jnp.where(me < near, -1.0, 1.0)
+    taps = jnp.concatenate([filt[:, :, part].reshape(SIDE, LANES) for part in range(parts)], axis=1)
+    mixed = mul(first_all[...], stack_right(taps))
+    tap_re, tap_im = spectrum(twisted(mixed[:, :LANES], 0), twisted(mixed[:, LANES:], 1))
+    tap_im = tap_im * jnp.where(me < near, -1.0, 1.0)
 
     for copy in side_copies:
         copy.wait_recv()
-    side_total = part_spectrum(0, side[:, 0].reshape(depth, LANES))
-    for part in range(1, parts):
-        side_total += part_spectrum(part, side[:, part].reshape(depth, LANES))
-    joined = product(side_total, tap_re, -tap_im)
-    for part in range(parts):
-        side_result[:, part] = part_tokens(part, joined, 0).reshape(near, *side_result.shape[2:])
+    tokens = jnp.concatenate([side[:, part].reshape(depth, LANES) for part in range(parts)], axis=1)
+    held = jnp.concatenate([first_all[:, third * SIDE:third * SIDE + depth] for third in range(3)], axis=1)
+    mixed = mul(held, stack_right(tokens))
+    side_re, side_im = spectrum(twisted(mixed[:, :LANES], 0), twisted(mixed[:, LANES:], 1))
+    level = jnp.concatenate(levels(side_re, side_im, tap_re, -tap_im), axis=1)
+    rebuilt = mul(last_all[:depth], stack_right(level))
+    for part in range(parts):
+        side_result[:, part] = rebuilt[:, part * LANES:(part + 1) * LANES].reshape(near, *side_result.shape[2:])
     for step in range(1, near):
         target = lax.rem(me + step, near)
         copy = pltpu.make_async_remote_copy(
@@ -213,12 +225,11 @@
         home_copies.append(copy)
     back[me] = side_result[local]
 
-    for part in range(1, parts):
-        row_total += row_spectrum(part)
-    joined = product(row_total, tap_re, tap_im)
+    row_re, row_im = spectrum(row_near, row_part(1))
+    kept = pl.ds(pl.multiple_of((me // near) * depth, depth), depth)
     place = lax.rem(me + near, blocks)
-    for part in range(parts):
-        result[part] = part_tokens(part, joined, pl.multiple_of((me // near) * depth, depth)).reshape(result.shape[1:])
+    for part, level in enumerate(levels(row_re, row_im, tap_re, tap_im)):
+        result[part] = mul(last_all[kept, :], stack_right(level)).reshape(result.shape[1:])
         for step in range(1, near):
             target = lax.rem(me + step, near)
             copy = pltpu.make_async_remote_copy(
@@ -265,14 +276,10 @@
             pltpu.VMEM((parts, near, high, LANES), f32),
             pltpu.VMEM((near, parts, high, LANES), f32),
             pltpu.VMEM((blocks, parts, high, LANES), f32),
-            pltpu.VMEM((2 * SIDE, SIDE), bf16),
-            pltpu.VMEM((2 * SIDE, SIDE), bf16),
-            pltpu.VMEM((2 * SIDE, 2 * SIDE), bf16),
-            pltpu.VMEM((2 * SIDE, 2 * SIDE), bf16),
-            pltpu.VMEM((parts, 2 * SIDE, SIDE), bf16),
-            pltpu.VMEM((parts, 2 * SIDE, SIDE), bf16),
-            pltpu.VMEM((SIDE, 2 * SIDE), bf16),
-            pltpu.VMEM((SIDE, 2 * SIDE), bf16),
+            pltpu.VMEM((2 * SIDE, 3 * SIDE), bf16),
+            pltpu.VMEM((3 * SIDE, SIDE), bf16),
+            pltpu.VMEM((3 * SIDE, SIDE), bf16),
+            pltpu.VMEM((SIDE, 6 * SIDE), bf16),
             pltpu.SemaphoreType.DMA((len(operands),)),
             pltpu.SemaphoreType.DMA((blocks,)),
             pltpu.SemaphoreType.DMA((blocks,)),

time: 28.1 us -> 26.5 us (0.943)
  Pallas kernels: 25.4 us -> 23.8 us
    pallas_call x1, Pallas kernels: 25.4 us -> 23.8 us  [rows_on_device(): pl.pallas_call(partial(row_kernel, blocks, groups), out_shape=jax.ShapeDt...]
where the time goes in v1:
time: 26.5 us; the launch traced here: 26.3 us
  Pallas kernels  23.8 us (90%)
  other arithmetic  1.83 us (7%)
  between operations  0.69 us (3%)
    pallas_call x1, Pallas kernels, rows_on_device(): pl.pallas_call(partial(row_kernel, blocks, groups), out_shape=jax.ShapeDt...  23.8 us
    mul x1, other arithmetic, rows_on_device(): gated_grad * key_gate  1.83 us

profile of v1, /device:TPU:0, one launch (start us, length us, event | category | flops | bytes accessed | tf_op | source)
XLA Modules:
  0.0 26.3 jit_solution(4700769491715553367)
XLA Ops:
  0.6 0.0 copy-start.2
  0.6 0.0 copy-start.1
  0.7 0.0 copy-start
  0.7 23.8 %shard_map.139 = f32[8,8192]{1,0:T(8,128)} custom-call(f32[4,8192]{1,0:T(4,128)} %k_hbm.1, f32[4,8192]{1,0:T(4,128)} %v_hbm.1, f32[4,8192]{1,0:T(4,128)} %q_hbm.1, f32[4,8192]{1,0:T(4,128)} %c_hbm.1, f32[4,2048]{1,0:T(4,128)} %taps_hbm.1, f32[512,256]{1,0:T(8,128)} %constant.14.clone.first_hbm, f32[256,256]{1,0:T(8,128)} %constant.15.clone.mid_hbm, ...), custom_call_target="tpu_custom_call" | custom-call | tf_op jit(solution)/shard_map/pallas_call | solution.py:264
  24.5 0.0 copy-done.2
  24.5 0.0 copy-done.1
  24.5 0.0 copy-done
  24.5 1.8 %slice_multiply_fusion.1 = (f32[4,8192]{1,0:T(4,128)}, f32[4,8192]{1,0:T(4,128)}, f32[4,8192]{1,0:T(4,128)}) fusion(f32[4,8192]{1,0:T(4,128)S(1)} %copy-done, f32[8,8192]{1,0:T(8,128)} %shard_map.139, f32[4,8192]{1,0:T(4,128)S(1)} %copy-done.1, f32[4,8192]{1,0:T(4,128)S(1)} %copy-done.2), kind=kLoop, calls=%fused_computation.1 | loop fusion | flops 98304 | bytes 1048576 | tf_op jit(solution)/shard_map/mul | solution.py:299
Async XLA Ops:
  0.6 23.8 %copy-start.2 = (f32[4,8192]{1,0:T(4,128)S(1)}, f32[4,8192]{1,0:T(4,128)}, u32[]{:S(2)}) copy-start(f32[4,8192]{1,0:T(4,128)} %c_hbm.1) | copy-start | bytes 393220
  0.6 23.8 %copy-start.1 = (f32[4,8192]{1,0:T(4,128)S(1)}, f32[4,8192]{1,0:T(4,128)}, u32[]{:S(2)}) copy-start(f32[4,8192]{1,0:T(4,128)} %v_hbm.1) | copy-start | bytes 393220
  0.7 23.8 %copy-start = (f32[4,8192]{1,0:T(4,128)S(1)}, f32[4,8192]{1,0:T(4,128)}, u32[]{:S(2)}) copy-start(f32[4,8192]{1,0:T(4,128)} %k_hbm.1) | copy-start | bytes 393220

commit v2 on v1

--- a/solution.py
+++ b/solution.py
@@ -93,18 +93,9 @@
     for part in range(parts):
         for row in range(taps_ref.shape[1] // SIDE):
             tap_pieces[:, part, row, :] = taps_ref[:, span(row, part)]
-    for load in loads[1:5]:
-        load.wait()
-    for part in range(parts):
-        for row in range(k_ref.shape[1] // SIDE):
-            tokens = span(row, part)
-            pieces[:count, part, row, :] = k_ref[:, tokens] * v_ref[:, tokens]
-            pieces[count:, part, row, :] = c_ref[:, tokens] * q_ref[:, tokens]
-
-    pl.semaphore_wait(barrier, blocks + groups - 2)
-
     tap_copies, slab_copies, side_copies, home_copies = [], [], [], []
     in_copies, out_copies = [[] for _ in range(parts)], [[] for _ in range(parts)]
+    pl.semaphore_wait(barrier, blocks + groups - 2)
     for step in range(1, blocks):
         target = lax.rem(me + step, blocks)
         copy = pltpu.make_async_remote_copy(
@@ -114,7 +105,23 @@
         )
         copy.start()
         tap_copies.append(copy)
+
+    for load in loads[1:5]:
+        load.wait()
     for part in range(parts):
+        for row in range(k_ref.shape[1] // SIDE):
+            tokens = span(row, part)
+            pieces[:count, part, row, :] = k_ref[:, tokens] * v_ref[:, tokens]
+            pieces[count:, part, row, :] = c_ref[:, tokens] * q_ref[:, tokens]
+        for step in range(1, near if part == parts - 1 else 1):
+            target = base + lax.rem(me + step, near)
+            copy = pltpu.make_async_remote_copy(
+                src_ref=pieces.at[target], dst_ref=side.at[local],
+                send_sem=side_send.at[step], recv_sem=side_recv.at[step],
+                device_id=(target, col), device_id_type=MESH,
+            )
+            copy.start()
+            side_copies.append(copy)
         for step in range(1, blocks):
             target = lax.rem(me + step, blocks)
             copy = pltpu.make_async_remote_copy(
@@ -124,15 +131,6 @@
             )
             copy.start()
             in_copies[part].append(copy)
-        for step in range(1, near if part == 0 else 1):
-            target = base + lax.rem(me + step, near)
-            copy = pltpu.make_async_remote_copy(
-                src_ref=pieces.at[target], dst_ref=side.at[local],
-                send_sem=side_send.at[step], recv_sem=side_recv.at[step],
-                device_id=(target, col), device_id_type=MESH,
-            )
-            copy.start()
-            side_copies.append(copy)
     side[local] = pieces[me]
     filt[me, col] = tap_pieces[lax.rem(me, count)]
     for part in range(parts):
@@ -197,6 +195,12 @@
         return twisted(mul(first_all[...], stack_right(rows[part].reshape(SIDE, LANES))), part)
 
     row_near = row_part(0)
+    for copy in side_copies:
+        copy.wait_recv()
+    tokens = jnp.concatenate([side[:, part].reshape(depth, LANES) for part in range(parts)], axis=1)
+    held = jnp.concatenate([first_all[:, third * SIDE:third * SIDE + depth] for third in range(3)], axis=1)
+    mixed = mul(held, stack_right(tokens))
+    side_re, side_im = spectrum(twisted(mixed[:, :LANES], 0), twisted(mixed[:, LANES:], 1))
     for copy in slab_copies:
         copy.wait_recv()
     taps = jnp.concatenate([filt[:, :, part].reshape(SIDE, LANES) for part in range(parts)], axis=1)
@@ -204,12 +208,6 @@
     tap_re, tap_im = spectrum(twisted(mixed[:, :LANES], 0), twisted(mixed[:, LANES:], 1))
     tap_im = tap_im * jnp.where(me < near, -1.0, 1.0)
 
-    for copy in side_copies:
-        copy.wait_recv()
-    tokens = jnp.concatenate([side[:, part].reshape(depth, LANES) for part in range(parts)], axis=1)
-    held = jnp.concatenate([first_all[:, third * SIDE:third * SIDE + depth] for third in range(3)], axis=1)
-    mixed = mul(held, stack_right(tokens))
-    side_re, side_im = spectrum(twisted(mixed[:, :LANES], 0), twisted(mixed[:, LANES:], 1))
     level = jnp.concatenate(levels(side_re, side_im, tap_re, -tap_im), axis=1)
     rebuilt = mul(last_all[:depth], stack_right(level))
     for part in range(parts):

time: 26.5 us -> 26.1 us (0.985)
  Pallas kernels: 23.8 us -> 23.4 us
    pallas_call x1, Pallas kernels: 23.8 us -> 23.4 us  [rows_on_device(): pl.pallas_call(partial(row_kernel, blocks, groups), out_shape=jax.ShapeDt...]
where the time goes in v2:
time: 26.1 us; the launch traced here: 26 us
  Pallas kernels  23.4 us (90%)
  other arithmetic  1.83 us (7%)
  between operations  0.69 us (3%)
    pallas_call x1, Pallas kernels, rows_on_device(): pl.pallas_call(partial(row_kernel, blocks, groups), out_shape=jax.ShapeDt...  23.4 us
    mul x1, other arithmetic, rows_on_device(): gated_grad * key_gate  1.83 us

profile of v2, /device:TPU:0, one launch (start us, length us, event | category | flops | bytes accessed | tf_op | source)
XLA Modules:
  0.0 26.0 jit_solution(16027705172618562579)
XLA Ops:
  0.6 0.0 copy-start.2
  0.6 0.0 copy-start.1
  0.7 0.0 copy-start
  0.7 23.4 %shard_map.139 = f32[8,8192]{1,0:T(8,128)} custom-call(f32[4,8192]{1,0:T(4,128)} %k_hbm.1, f32[4,8192]{1,0:T(4,128)} %v_hbm.1, f32[4,8192]{1,0:T(4,128)} %q_hbm.1, f32[4,8192]{1,0:T(4,128)} %c_hbm.1, f32[4,2048]{1,0:T(4,128)} %taps_hbm.1, f32[512,256]{1,0:T(8,128)} %constant.14.clone.first_hbm, f32[256,256]{1,0:T(8,128)} %constant.15.clone.mid_hbm, ...), custom_call_target="tpu_custom_call" | custom-call | tf_op jit(solution)/shard_map/pallas_call | solution.py:262
  24.1 0.0 copy-done.2
  24.1 0.0 copy-done.1
  24.1 0.0 copy-done
  24.1 1.8 %slice_multiply_fusion.1 = (f32[4,8192]{1,0:T(4,128)}, f32[4,8192]{1,0:T(4,128)}, f32[4,8192]{1,0:T(4,128)}) fusion(f32[4,8192]{1,0:T(4,128)S(1)} %copy-done, f32[8,8192]{1,0:T(8,128)} %shard_map.139, f32[4,8192]{1,0:T(4,128)S(1)} %copy-done.1, f32[4,8192]{1,0:T(4,128)S(1)} %copy-done.2), kind=kLoop, calls=%fused_computation.1 | loop fusion | flops 98304 | bytes 1048576 | tf_op jit(solution)/shard_map/mul | solution.py:297
Async XLA Ops:
  0.6 23.5 %copy-start.2 = (f32[4,8192]{1,0:T(4,128)S(1)}, f32[4,8192]{1,0:T(4,128)}, u32[]{:S(2)}) copy-start(f32[4,8192]{1,0:T(4,128)} %c_hbm.1) | copy-start | bytes 393220
  0.6 23.5 %copy-start.1 = (f32[4,8192]{1,0:T(4,128)S(1)}, f32[4,8192]{1,0:T(4,128)}, u32[]{:S(2)}) copy-start(f32[4,8192]{1,0:T(4,128)} %v_hbm.1) | copy-start | bytes 393220
  0.7 23.5 %copy-start = (f32[4,8192]{1,0:T(4,128)S(1)}, f32[4,8192]{1,0:T(4,128)}, u32[]{:S(2)}) copy-start(f32[4,8192]{1,0:T(4,128)} %k_hbm.1) | copy-start | bytes 393220

commit v3 on v2

--- a/solution.py
+++ b/solution.py
@@ -70,6 +70,7 @@
     base = (me // near) * near
     local = lax.rem(me, near)
     depth = SIDE // 2
+    far_first = sorted(range(1, blocks), key=lambda step: abs(step - near))
 
     sources = (taps_hbm, k_hbm, v_hbm, c_hbm, q_hbm, first_hbm, mid_hbm, inv_hbm, turn_re_hbm, turn_im_hbm, last_hbm, shift_hbm)
     targets = (taps_ref, k_ref, v_ref, c_ref, q_ref, first_ref, mid_ref, inv_ref, turn_re_ref, turn_im_ref, last_ref, shift_ref)
@@ -96,7 +97,7 @@
     tap_copies, slab_copies, side_copies, home_copies = [], [], [], []
     in_copies, out_copies = [[] for _ in range(parts)], [[] for _ in range(parts)]
     pl.semaphore_wait(barrier, blocks + groups - 2)
-    for step in range(1, blocks):
+    for step in far_first:
         target = lax.rem(me + step, blocks)
         copy = pltpu.make_async_remote_copy(
             src_ref=tap_pieces.at[lax.rem(target, count)], dst_ref=filt.at[me, col],
@@ -113,6 +114,15 @@
             tokens = span(row, part)
             pieces[:count, part, row, :] = k_ref[:, tokens] * v_ref[:, tokens]
             pieces[count:, part, row, :] = c_ref[:, tokens] * q_ref[:, tokens]
+        for step in far_first[:near - 1]:
+            target = lax.rem(me + step, blocks)
+            copy = pltpu.make_async_remote_copy(
+                src_ref=pieces.at[lax.rem(target + near, blocks), part], dst_ref=rows.at[part, me],
+                send_sem=in_send.at[part, step], recv_sem=in_recv.at[part, step],
+                device_id=(target, col), device_id_type=MESH,
+            )
+            copy.start()
+            in_copies[part].append(copy)
         for step in range(1, near if part == parts - 1 else 1):
             target = base + lax.rem(me + step, near)
             copy = pltpu.make_async_remote_copy(
@@ -122,7 +132,7 @@
             )
             copy.start()
             side_copies.append(copy)
-        for step in range(1, blocks):
+        for step in far_first[near - 1:]:
             target = lax.rem(me + step, blocks)
             copy = pltpu.make_async_remote_copy(
                 src_ref=pieces.at[lax.rem(target + near, blocks), part], dst_ref=rows.at[part, me],

time: 26.1 us -> 26.8 us (1.027)
  Pallas kernels: 23.4 us -> 24.1 us
    pallas_call x1, Pallas kernels: 23.4 us -> 24.1 us  [rows_on_device(): pl.pallas_call(partial(row_kernel, blocks, groups), out_shape=jax.ShapeDt...]
where the time goes in v3:
time: 26.8 us; the launch traced here: 26.7 us
  Pallas kernels  24.1 us (90%)
  other arithmetic  1.83 us (7%)
  between operations  0.69 us (3%)
    pallas_call x1, Pallas kernels, rows_on_device(): pl.pallas_call(partial(row_kernel, blocks, groups), out_shape=jax.ShapeDt...  24.1 us
    mul x1, other arithmetic, rows_on_device(): gated_grad * key_gate  1.83 us

profile of v3, /device:TPU:0, one launch (start us, length us, event | category | flops | bytes accessed | tf_op | source)
XLA Modules:
  0.0 26.7 jit_solution(4954485639358619713)
XLA Ops:
  0.6 0.0 copy-start.2
  0.6 0.0 copy-start.1
  0.7 0.0 copy-start
  0.7 24.1 %shard_map.139 = f32[8,8192]{1,0:T(8,128)} custom-call(f32[4,8192]{1,0:T(4,128)} %k_hbm.1, f32[4,8192]{1,0:T(4,128)} %v_hbm.1, f32[4,8192]{1,0:T(4,128)} %q_hbm.1, f32[4,8192]{1,0:T(4,128)} %c_hbm.1, f32[4,2048]{1,0:T(4,128)} %taps_hbm.1, f32[512,256]{1,0:T(8,128)} %constant.14.clone.first_hbm, f32[256,256]{1,0:T(8,128)} %constant.15.clone.mid_hbm, ...), custom_call_target="tpu_custom_call" | custom-call | tf_op jit(solution)/shard_map/pallas_call | solution.py:272
  24.8 0.0 copy-done.2
  24.8 0.0 copy-done.1
  24.8 0.0 copy-done
  24.8 1.8 %slice_multiply_fusion.1 = (f32[4,8192]{1,0:T(4,128)}, f32[4,8192]{1,0:T(4,128)}, f32[4,8192]{1,0:T(4,128)}) fusion(f32[4,8192]{1,0:T(4,128)S(1)} %copy-done, f32[8,8192]{1,0:T(8,128)} %shard_map.139, f32[4,8192]{1,0:T(4,128)S(1)} %copy-done.1, f32[4,8192]{1,0:T(4,128)S(1)} %copy-done.2), kind=kLoop, calls=%fused_computation.1 | loop fusion | flops 98304 | bytes 1048576 | tf_op jit(solution)/shard_map/mul | solution.py:307
Async XLA Ops:
  0.6 24.2 %copy-start.2 = (f32[4,8192]{1,0:T(4,128)S(1)}, f32[4,8192]{1,0:T(4,128)}, u32[]{:S(2)}) copy-start(f32[4,8192]{1,0:T(4,128)} %c_hbm.1) | copy-start | bytes 393220
  0.6 24.2 %copy-start.1 = (f32[4,8192]{1,0:T(4,128)S(1)}, f32[4,8192]{1,0:T(4,128)}, u32[]{:S(2)}) copy-start(f32[4,8192]{1,0:T(4,128)} %v_hbm.1) | copy-start | bytes 393220
  0.7 24.2 %copy-start = (f32[4,8192]{1,0:T(4,128)S(1)}, f32[4,8192]{1,0:T(4,128)}, u32[]{:S(2)}) copy-start(f32[4,8192]{1,0:T(4,128)} %k_hbm.1) | copy-start | bytes 393220

commit v4 on v2

--- a/solution.py
+++ b/solution.py
@@ -58,7 +58,7 @@
     first_hbm, mid_hbm, inv_hbm, last_hbm, turn_re_hbm, turn_im_hbm, shift_hbm, out_ref,
     k_ref, v_ref, q_ref, c_ref, taps_ref, first_ref, mid_ref, inv_ref, last_ref, turn_re_ref, turn_im_ref, shift_ref,
     pieces, tap_pieces, rows, side, filt, result, side_result, back,
-    first_all, mid_all, inv_all, last_all,
+    first_all, mid_all, inv_all, last_all, staged, store_sem,
     load_sem, tap_send, tap_recv, slab_send, slab_recv, in_send, in_recv, out_send, out_recv,
     side_send, side_recv, home_send, home_recv,
 ):
@@ -238,13 +238,23 @@
             copy.start()
             out_copies[part].append(copy)
         back[place, part] = result[part, local]
+    half = me // near
     for copy in home_copies:
         copy.wait_recv()
+    for part in range(parts):
+        for row in range(back.shape[2]):
+            staged[half, :, span(row, part)] = back[pl.ds(half * count, count), part, row, :]
+    side_store = pltpu.make_async_copy(staged.at[half], out_ref.at[half], store_sem.at[0])
+    side_store.start()
     for part in range(parts):
         for copy in out_copies[part]:
             copy.wait_recv()
         for row in range(back.shape[2]):
-            out_ref[:, span(row, part)] = back[:, part, row, :]
+            staged[1 - half, :, span(row, part)] = back[pl.ds((1 - half) * count, count), part, row, :]
+    main_store = pltpu.make_async_copy(staged.at[1 - half], out_ref.at[1 - half], store_sem.at[1])
+    main_store.start()
+    side_store.wait()
+    main_store.wait()
     for copy in tap_copies + sum(in_copies, []) + slab_copies + side_copies + home_copies + sum(out_copies, []):
         copy.wait_send()
 
@@ -261,9 +271,9 @@
     operands = (key_gate, value_input, query_gate, cotangent, filter_taps, *[jnp.asarray(table) for table in tables])
     sums = pl.pallas_call(
         partial(row_kernel, blocks, groups),
-        out_shape=jax.ShapeDtypeStruct((blocks, width), f32),
+        out_shape=jax.ShapeDtypeStruct((2, count, width), f32),
         in_specs=[pl.BlockSpec(memory_space=pl.ANY)] * len(operands),
-        out_specs=pl.BlockSpec(memory_space=pltpu.VMEM),
+        out_specs=pl.BlockSpec(memory_space=pl.ANY),
         scratch_shapes=[
             *[pltpu.VMEM(operand.shape, f32) for operand in operands],
             pltpu.VMEM((blocks, parts, high, LANES), f32),
@@ -278,6 +288,8 @@
             pltpu.VMEM((3 * SIDE, SIDE), bf16),
             pltpu.VMEM((3 * SIDE, SIDE), bf16),
             pltpu.VMEM((SIDE, 6 * SIDE), bf16),
+            pltpu.VMEM((2, count, width), f32),
+            pltpu.SemaphoreType.DMA((2,)),
             pltpu.SemaphoreType.DMA((len(operands),)),
             pltpu.SemaphoreType.DMA((blocks,)),
             pltpu.SemaphoreType.DMA((blocks,)),
@@ -293,7 +305,7 @@
             collective_id=0, has_side_effects=True, vmem_limit_bytes=VMEM_BYTES
         ),
     )(*operands)
-    convolved, gated_grad = sums[:count], sums[count:]
+    convolved, gated_grad = sums[0], sums[1]
     return (cotangent * convolved, gated_grad * value_input, gated_grad * key_gate)
 
 

time: 26.1 us -> 26 us (level)
  no operation moved by 1% of the time
where the time goes in v4:
time: 26 us; the launch traced here: 25.8 us
  Pallas kernels  23.4 us (90%)
  other arithmetic  1.76 us (7%)
  between operations  0.69 us (3%)
    pallas_call x1, Pallas kernels, rows_on_device(): pl.pallas_call(partial(row_kernel, blocks, groups), out_shape=jax.ShapeDt...  23.4 us
    mul x1, other arithmetic, rows_on_device(): gated_grad * key_gate  1.76 us

profile of v4, /device:TPU:0, one launch (start us, length us, event | category | flops | bytes accessed | tf_op | source)
XLA Modules:
  0.0 25.8 jit_solution(7634721324287185438)
XLA Ops:
  0.6 0.0 copy-start.2
  0.6 0.0 copy-start.1
  0.7 0.0 copy-start
  0.7 23.4 %shard_map.139 = f32[2,4,8192]{2,1,0:T(4,128)} custom-call(f32[4,8192]{1,0:T(4,128)} %k_hbm.1, f32[4,8192]{1,0:T(4,128)} %v_hbm.1, f32[4,8192]{1,0:T(4,128)} %q_hbm.1, f32[4,8192]{1,0:T(4,128)} %c_hbm.1, f32[4,2048]{1,0:T(4,128)} %taps_hbm.1, f32[512,256]{1,0:T(8,128)} %constant.14.clone.first_hbm, f32[256,256]{1,0:T(8,128)} %constant.15.clone.mid_hbm, ...), custom_call_target="tpu_custom_call" | custom-call | tf_op jit(solution)/shard_map/pallas_call | solution.py:272
  24.0 0.0 copy-done.2
  24.0 0.0 copy-done.1
  24.1 0.0 copy-done
  24.1 1.8 %bitcast_multiply_fusion = (f32[4,8192]{1,0:T(4,128)}, f32[4,8192]{1,0:T(4,128)}, f32[4,8192]{1,0:T(4,128)}) fusion(f32[4,8192]{1,0:T(4,128)S(1)} %copy-done, f32[2,4,8192]{2,1,0:T(4,128)} %shard_map.139, f32[4,8192]{1,0:T(4,128)S(1)} %copy-done.1, f32[4,8192]{1,0:T(4,128)S(1)} %copy-done.2), kind=kLoop, calls=%fused_computation | loop fusion | flops 98304 | bytes 1048576 | tf_op jit(solution)/shard_map/mul | solution.py:309
Async XLA Ops:
  0.6 23.4 %copy-start.2 = (f32[4,8192]{1,0:T(4,128)S(1)}, f32[4,8192]{1,0:T(4,128)}, u32[]{:S(2)}) copy-start(f32[4,8192]{1,0:T(4,128)} %c_hbm.1) | copy-start | bytes 393220
  0.6 23.4 %copy-start.1 = (f32[4,8192]{1,0:T(4,128)S(1)}, f32[4,8192]{1,0:T(4,128)}, u32[]{:S(2)}) copy-start(f32[4,8192]{1,0:T(4,128)} %v_hbm.1) | copy-start | bytes 393220
  0.7 23.4 %copy-start = (f32[4,8192]{1,0:T(4,128)S(1)}, f32[4,8192]{1,0:T(4,128)}, u32[]{:S(2)}) copy-start(f32[4,8192]{1,0:T(4,128)} %k_hbm.1) | copy-start | bytes 393220
